TPU v7x, 256 devices: a whole 4x4x8 slice. The times are simulated.
256 devices in a mesh: grp: 128 (over x, y, z), rep: 2 (over core).
Axes of the slice: x: 4, y: 4, z: 8, core: 2. Of those that a mesh axis runs over, the one named last changes fastest.
Arguments:
- samples: bfloat16 [1024, 1097728], P(('grp', 'rep')), as said below
- fir_coeffs: float32 [4, 16384], replicated, may hold values from 0.2 to 1
- kept_channels: int32 [256], replicated, may hold values from 0 to 8191, as said below
- usable: int32 [1024], replicated, may hold values 0 or 1
- initial_gains: float32 [256, 2, 1024], P(('grp', 'rep')), as said below
Outputs:
- solved_gains: float32 [256, 2, 1024], P(('grp', 'rep'))
- bandpass: float32 [256, 2, 1024], P(('grp', 'rep'))
Inputs may be any that keep to these rules, and one draw needn't show every extreme that they name: Real samples of each input, frame after frame. `kept_channels`: strictly increasing; entry j lies in [j * 32, (j + 1) * 32). `initial_gains`: complex starting gains.
All inputs are finite; a program needn't handle non-finite values.
Results may differ from a plain program's by a relative error of at most 0.004.
Values may be sent and summed in bfloat16 or wider, within the bound.
A program may use at most 128 MiB of HBM per device.

v0:
```python
import math

import jax
import jax.numpy as jnp
from jax import lax
from jax.sharding import PartitionSpec as P

CHAN = 8192
ITERS = 4
POLY = 8


def legendre_basis(kept_channels):
    coord = kept_channels.astype(jnp.float32) * (2.0 / (CHAN - 1)) - 1.0
    columns = [jnp.ones_like(coord), coord]
    for order in range(1, POLY - 1):
        columns.append(
            ((2 * order + 1) * coord * columns[order] - order * columns[order - 1]) / (order + 1)
        )
    return jnp.stack(columns[:POLY], axis=1)


def solve_gram(gram, moments):
    factor = jnp.linalg.cholesky(gram)
    forward = []
    for row in range(POLY):
        value = moments[row]
        for col in range(row):
            value = value - factor[row, col] * forward[col]
        forward.append(value / factor[row, row])
    backward = [None] * POLY
    for row in range(POLY - 1, -1, -1):
        value = forward[row]
        for col in range(row + 1, POLY):
            value = value - factor[col, row] * backward[col]
        backward[row] = value / factor[row, row]
    return jnp.stack(backward, axis=0)


def calibrate(vis_re, vis_im, power, usable_f, gains):
    scale = lax.rsqrt(power + 1e-06) * usable_f
    weight = scale[:, None] * scale[None, :] * (1.0 - jnp.eye(scale.shape[0], dtype=jnp.float32))
    w_re = vis_re * weight[None]
    w_im = vis_im * weight[None]
    g_re = gains[:, 0]
    g_im = gains[:, 1]
    for step in range(ITERS):
        both = jnp.stack([g_re, g_im], axis=2)
        from_re = jnp.einsum("cpq,cqk->cpk", w_re, both, precision=lax.Precision.HIGHEST)
        from_im = jnp.einsum("cpq,cqk->cpk", w_im, both, precision=lax.Precision.HIGHEST)
        num_re = from_re[:, :, 0] - from_im[:, :, 1]
        num_im = from_re[:, :, 1] + from_im[:, :, 0]
        magnitude = usable_f[None, :] * (g_re * g_re + g_im * g_im)
        total = jnp.sum(magnitude, axis=1, keepdims=True)
        denom = total - magnitude + 1e-06
        new_re = num_re / denom
        new_im = num_im / denom
        if step % 2 == 1:
            g_re = (new_re + g_re) / 2.0
            g_im = (new_im + g_im) / 2.0
        else:
            g_re = new_re
            g_im = new_im
    return jnp.stack([g_re, g_im], axis=1)


def per_device(samples, fir_coeffs, kept_channels, usable, initial_gains):
    inp_dev = samples.shape[0]
    taps = fir_coeffs.shape[0]
    nfft = fir_coeffs.shape[1]
    frames_total = samples.shape[1] // nfft
    spec = frames_total - taps + 1
    kept = kept_channels.shape[0]
    ch_dev = initial_gains.shape[0]
    n_grp = lax.axis_size("grp")
    n_rep = lax.axis_size("rep")
    inputs = inp_dev * n_grp * n_rep
    frames = samples.reshape(inp_dev, frames_total, nfft).astype(jnp.float32)
    filtered = fir_coeffs[0][None, None, :] * frames[:, 0:spec, :]
    for tap in range(1, taps):
        filtered = filtered + fir_coeffs[tap][None, None, :] * frames[:, tap : tap + spec, :]
    filtered = filtered.astype(jnp.bfloat16).reshape(inp_dev * spec, nfft)
    width = min(4096, nfft)
    step_angle = jnp.float32(2.0 * math.pi / nfft)

    def transform_block(index, carry):
        acc_re, acc_im = carry
        start = index * width
        piece = lax.dynamic_slice_in_dim(filtered, start, width, 1)
        sample_index = start + lax.iota(jnp.int32, width)
        phase = kept_channels[:, None] * sample_index[None, :] % nfft
        angle = phase.astype(jnp.float32) * step_angle
        table_re = jnp.cos(angle).astype(jnp.bfloat16)
        table_im = (-jnp.sin(angle)).astype(jnp.bfloat16)
        acc_re = acc_re + jnp.einsum(
            "kw,rw->kr", table_re, piece, preferred_element_type=jnp.float32
        )
        acc_im = acc_im + jnp.einsum(
            "kw,rw->kr", table_im, piece, preferred_element_type=jnp.float32
        )
        return (acc_re, acc_im)

    empty = jnp.zeros((kept, inp_dev * spec), jnp.float32)
    real_part, imag_part = lax.fori_loop(0, nfft // width, transform_block, (empty, empty))
    spectra = jnp.stack(
        [real_part.reshape(kept, inp_dev, spec), imag_part.reshape(kept, inp_dev, spec)], axis=2
    )
    spectra = spectra.reshape(kept, inp_dev * 2 * spec).astype(jnp.bfloat16)
    turned = lax.all_to_all(
        lax.all_to_all(spectra, "grp", split_axis=0, concat_axis=1, tiled=True),
        "rep",
        split_axis=0,
        concat_axis=1,
        tiled=True,
    )
    turned = turned.reshape(ch_dev, n_rep, n_grp, inp_dev, 2 * spec)
    stacked = jnp.transpose(turned, (0, 2, 1, 3, 4)).reshape(ch_dev, inputs, 2 * spec)
    other = jnp.concatenate([stacked[:, :, spec:], -stacked[:, :, :spec]], axis=2)
    vis_re = jnp.einsum("cps,cqs->cpq", stacked, stacked, preferred_element_type=jnp.float32) / spec
    vis_im = jnp.einsum("cps,cqs->cpq", stacked, other, preferred_element_type=jnp.float32) / spec
    autos = jnp.diagonal(vis_re, axis1=1, axis2=2)
    power = lax.psum(jnp.sum(autos, axis=0), ("grp", "rep")) / kept
    usable_f = usable.astype(jnp.float32)
    solved = calibrate(vis_re, vis_im, power, usable_f, initial_gains)
    basis = legendre_basis(kept_channels)
    gram = jnp.dot(basis.T, basis, precision=lax.Precision.HIGHEST)
    first = lax.axis_index(("grp", "rep")) * ch_dev
    own_basis = lax.dynamic_slice_in_dim(basis, first, ch_dev, 0)
    everything = lax.all_gather(solved, ("grp", "rep"), axis=0, tiled=True)
    moments = jnp.dot(
        basis.T, everything.reshape(kept, 2 * inputs), precision=lax.Precision.HIGHEST
    )
    coeffs = solve_gram(gram, moments)
    bandpass = jnp.dot(own_basis, coeffs, precision=lax.Precision.HIGHEST).reshape(
        ch_dev, 2, inputs
    )
    return (solved, bandpass)


def solution(mesh):
    placed = (P(("grp", "rep"), None), P(), P(), P(), P(("grp", "rep"), None, None))
    return jax.shard_map(
        per_device,
        mesh=mesh,
        in_specs=placed,
        out_specs=(P(("grp", "rep"), None, None), P(("grp", "rep"), None, None)),
        check_vma=False,
    )
```

profile of v0, /device:TPU:1, one launch (start us, length us, event | category | flops | bytes accessed | tf_op | source)
XLA Modules:
  0.0 541.8 jit_solution(6776984343551157011)
XLA Ops:
  7.2 1.6 fusion.77
  8.8 14.5 %reshape.241 = f32[4,67,16384]{2,1,0:T(8,128)} reshape(bf16[4,1097728]{1,0:T(4,128)(2,1)} %param.7) | data formatting | bytes 26345472 | tf_op jit(solution)/shard_map/convert_element_type | solution.py:78
  23.4 27.9 %fusion.24 = bf16[4,64,16384]{2,1,0:T(8,128)(2,1)} fusion(f32[4,67,16384]{2,1,0:T(8,128)} %reshape.241, f32[16384]{0:T(1024)S(1)} %bitcast.151, f32[16384]{0:T(1024)S(1)} %bitcast.152, f32[16384]{0:T(1024)S(1)} %bitcast.150, f32[16384]{0:T(1024)S(1)} %bitcast.149), kind=kLoop, calls=%fused_computation.28 | loop fusion | flops 33554432 | bytes 75759616 | tf_op jit(solution)/shard_map/convert_element_type | solution.py:82
  51.3 166.7 %while.18 = (s32[]{:T(128)}, f32[256,256]{1,0:T(8,128)S(1)}, f32[256,256]{1,0:T(8,128)S(1)}, s32[256]{0:T(256)S(1)}, bf16[256,16384]{1,0:T(8,128)(2,1)}, /*index=5*/s32[]{:T(128)}, s32[]{:T(128)}, s32[]{:T(128)}, s32[]{:T(128)}) while((s32[]{:T(128)}, f32[256,256]{1,0:T(8,128)S(1)}, f32[256,256]{1,0:T(8,128)S(1)}, ...), condition=%wide.region_1.2_spmd.clone, body=%wide.region_0.1_spmd.clone.sunk | while | flops 1106513920 | bytes 5294242 | solution.py:104
  73.4 17.4 %fusion.101 = f32[256,256]{1,0:T(8,128)S(1)} fusion(bf16[256,16384]{1,0:T(8,128)(2,1)} %get-tuple-element.310, s32[]{:T(128)S(6)} %select_n.66, s32[4096]{0:T(1024)S(1)} %iota_add_fusion.2, s32[256]{0:T(256)S(1)} %get-tuple-element.309, f32[256,256]{1,0:T(8,128)S(1)} %get-tuple-element.299, pred[]{:T(512)S(6)} %compare.11), kind=kOutput, calls=%fused_computation.15.clone.1 | convolution fusion | flops 553779200 | bytes 2638853 | tf_op jit(solution)/shard_map/while/body/eval_jaxpr/kw,rw->kr/dot_general | solution.py:98
  90.7 17.2 %fusion.100 = f32[256,256]{1,0:T(8,128)S(1)} fusion(bf16[256,16384]{1,0:T(8,128)(2,1)} %get-tuple-element.310, s32[]{:T(128)S(6)} %select_n.66, s32[4096]{0:T(1024)S(1)} %iota_add_fusion.2, s32[256]{0:T(256)S(1)} %get-tuple-element.309, f32[256,256]{1,0:T(8,128)S(1)} %get-tuple-element.298, pred[]{:T(512)S(6)} %compare.11), kind=kOutput, calls=%fused_computation.16.clone.1 | convolution fusion | flops 552730624 | bytes 2638853 | tf_op jit(solution)/shard_map/while/body/eval_jaxpr/kw,rw->kr/dot_general | solution.py:95
  108.0 17.4 %fusion.101 = f32[256,256]{1,0:T(8,128)S(1)} fusion(bf16[256,16384]{1,0:T(8,128)(2,1)} %get-tuple-element.310, s32[]{:T(128)S(6)} %select_n.66, s32[4096]{0:T(1024)S(1)} %iota_add_fusion.2, s32[256]{0:T(256)S(1)} %get-tuple-element.309, f32[256,256]{1,0:T(8,128)S(1)} %get-tuple-element.299, pred[]{:T(512)S(6)} %compare.11), kind=kOutput, calls=%fused_computation.15.clone.1 | convolution fusion | flops 553779200 | bytes 2638853 | tf_op jit(solution)/shard_map/while/body/eval_jaxpr/kw,rw->kr/dot_general | solution.py:98
  125.4 17.2 %fusion.100 = f32[256,256]{1,0:T(8,128)S(1)} fusion(bf16[256,16384]{1,0:T(8,128)(2,1)} %get-tuple-element.310, s32[]{:T(128)S(6)} %select_n.66, s32[4096]{0:T(1024)S(1)} %iota_add_fusion.2, s32[256]{0:T(256)S(1)} %get-tuple-element.309, f32[256,256]{1,0:T(8,128)S(1)} %get-tuple-element.298, pred[]{:T(512)S(6)} %compare.11), kind=kOutput, calls=%fused_computation.16.clone.1 | convolution fusion | flops 552730624 | bytes 2638853 | tf_op jit(solution)/shard_map/while/body/eval_jaxpr/kw,rw->kr/dot_general | solution.py:95
  142.6 17.4 %fusion.101 = f32[256,256]{1,0:T(8,128)S(1)} fusion(bf16[256,16384]{1,0:T(8,128)(2,1)} %get-tuple-element.310, s32[]{:T(128)S(6)} %select_n.66, s32[4096]{0:T(1024)S(1)} %iota_add_fusion.2, s32[256]{0:T(256)S(1)} %get-tuple-element.309, f32[256,256]{1,0:T(8,128)S(1)} %get-tuple-element.299, pred[]{:T(512)S(6)} %compare.11), kind=kOutput, calls=%fused_computation.15.clone.1 | convolution fusion | flops 553779200 | bytes 2638853 | tf_op jit(solution)/shard_map/while/body/eval_jaxpr/kw,rw->kr/dot_general | solution.py:98
  160.0 17.2 %fusion.100 = f32[256,256]{1,0:T(8,128)S(1)} fusion(bf16[256,16384]{1,0:T(8,128)(2,1)} %get-tuple-element.310, s32[]{:T(128)S(6)} %select_n.66, s32[4096]{0:T(1024)S(1)} %iota_add_fusion.2, s32[256]{0:T(256)S(1)} %get-tuple-element.309, f32[256,256]{1,0:T(8,128)S(1)} %get-tuple-element.298, pred[]{:T(512)S(6)} %compare.11), kind=kOutput, calls=%fused_computation.16.clone.1 | convolution fusion | flops 552730624 | bytes 2638853 | tf_op jit(solution)/shard_map/while/body/eval_jaxpr/kw,rw->kr/dot_general | solution.py:95
  177.2 17.4 %fusion.101 = f32[256,256]{1,0:T(8,128)S(1)} fusion(bf16[256,16384]{1,0:T(8,128)(2,1)} %get-tuple-element.310, s32[]{:T(128)S(6)} %select_n.66, s32[4096]{0:T(1024)S(1)} %iota_add_fusion.2, s32[256]{0:T(256)S(1)} %get-tuple-element.309, f32[256,256]{1,0:T(8,128)S(1)} %get-tuple-element.299, pred[]{:T(512)S(6)} %compare.11), kind=kOutput, calls=%fused_computation.15.clone.1 | convolution fusion | flops 553779200 | bytes 2638853 | tf_op jit(solution)/shard_map/while/body/eval_jaxpr/kw,rw->kr/dot_general | solution.py:98
  194.6 17.2 %fusion.100 = f32[256,256]{1,0:T(8,128)S(1)} fusion(bf16[256,16384]{1,0:T(8,128)(2,1)} %get-tuple-element.310, s32[]{:T(128)S(6)} %select_n.66, s32[4096]{0:T(1024)S(1)} %iota_add_fusion.2, s32[256]{0:T(256)S(1)} %get-tuple-element.309, f32[256,256]{1,0:T(8,128)S(1)} %get-tuple-element.298, pred[]{:T(512)S(6)} %compare.11), kind=kOutput, calls=%fused_computation.16.clone.1 | convolution fusion | flops 552730624 | bytes 2638853 | tf_op jit(solution)/shard_map/while/body/eval_jaxpr/kw,rw->kr/dot_general | solution.py:95
  218.0 0.1 copy.20
  218.1 0.1 copy.21
  218.2 0.4 copy.22
  218.7 1.0 convert_element_type.56
  219.7 16.3 %all-to-all-start = ((bf16[128,2,512]{2,1,0:T(2,128)(2,1)}), bf16[128,2,512]{2,1,0:T(2,128)(2,1)S(1)}, u32[]{:S(2)}, u32[]{:S(2)}) async-start(bf16[128,2,512]{2,1,0:T(2,128)(2,1)} %convert_element_type.56), calls=%async_computation | async-start | bytes 524288 | tf_op jit(solution)/shard_map/all_to_all | solution.py:110
  236.0 0.0 all-gather.2.cloned.1.call-start
  236.1 13.4 %all-to-all-done = bf16[128,2,512]{2,1,0:T(2,128)(2,1)S(1)} async-done(((bf16[128,2,512]{2,1,0:T(2,128)(2,1)}), bf16[128,2,512]{2,1,0:T(2,128)(2,1)S(1)}, u32[]{:S(2)}, u32[]{:S(2)}) %all-to-all-start) | async-done | bytes 262176 | tf_op jit(solution)/shard_map/all_to_all | solution.py:110
  249.5 0.5 broadcast.741
  250.0 1.4 reduce.17
  251.4 0.2 reshape.257
  251.6 6.1 %all_to_all.26 = bf16[2,2,32768]{2,1,0:T(2,128)(2,1)S(1)} all-to-all(bf16[2,2,32768]{2,1,0:T(2,128)(2,1)S(1)} %reshape.257), channel_id=1, replica_groups=mesh['grp'=128,'rep'=2] {'rep'}, dimensions={0} | all-to-all | bytes 524288 | tf_op jit(solution)/shard_map/all_to_all | solution.py:109
  257.7 0.3 reshape.258
  258.0 1.9 reduce.14
  259.9 0.2 reshape.229
  260.1 0.1 copy.24
  260.2 2.6 convolution_multiply_fusion
  262.9 17.3 %gather_fusion = f32[1024]{0:T(1024)S(1)} fusion(f32[1024,1024]{1,0:T(8,128)} %convolution_multiply_fusion, s32[1024]{0:T(1024)S(1)} %bitcast.138), kind=kCustom, calls=%fused_computation | custom fusion | bytes 16384 | tf_op jit(solution)/shard_map/jit(diagonal)/gather | solution.py:121
  280.2 72.9 %psum.7 = f32[1024]{0:T(1024)S(1)} all-reduce(f32[1024]{0:T(1024)S(1)} %gather_fusion), channel_id=1, replica_groups=mesh['grp'=128,'rep'=2] {'grp','rep'}, use_global_device_ids=true, to_apply=%region_2.3 | all-reduce | flops 1024 | bytes 8192 | tf_op jit(solution)/shard_map/psum | solution.py:122
  353.1 0.1 fusion.76
  353.3 0.6 fusion.61
  353.9 0.8 multiply_multiply_fusion
  354.7 0.8 copy-done
  355.4 4.0 convolution_bitcast_fusion.7
  359.4 3.6 convolution_bitcast_fusion.6
  363.1 1.3 fusion.62
  364.3 4.0 convolution_bitcast_fusion.5
  368.4 4.0 convolution_bitcast_fusion.4
  372.4 1.3 fusion.73
  373.6 4.0 convolution_bitcast_fusion.3
  377.7 3.6 convolution_bitcast_fusion.2
  381.3 1.3 fusion.63
  382.6 4.0 convolution_bitcast_fusion.1
  386.6 3.8 convolution_bitcast_fusion
  390.4 0.7 add_multiply_fusion.1
  391.0 0.6 pad_maximum_fusion.1
  391.8 0.1 fusion.81
  391.9 0.1 copy.26
  392.0 0.7 cholesky.18
  392.7 0.1 select_reduce_fusion
  392.7 0.6 compare_reduce_fusion
  393.4 0.6 select_select_fusion
  394.0 0.7 fusion.78
  396.0 0.2 dynamic-slice_reduce_fusion
  396.2 0.7 fusion.79
  397.0 93.6 %all-gather.2.cloned.1.call-done = f32[256,2,1024]{2,1,0:T(2,128)} async-done(((f32[1,2,1024]{2,1,0:T(2,128)}), f32[256,2,1024]{2,1,0:T(2,128)}) %all-gather.2.cloned.1.call-update) | async-done | bytes 2097168 | tf_op jit(solution)/shard_map/all_gather | solution.py:129
  490.5 2.5 copy.28
  493.0 1.1 fusion.80
  494.1 17.7 %subtract_divide_fusion.8 = (f32[1,2048]{1,0:T(1,128)S(1)}, f32[1,2048]{1,0:T(1,128)S(1)}, f32[1,2048]{1,0:T(1,128)S(1)}, f32[1,2048]{1,0:T(1,128)S(1)}, f32[1,2...) fusion(f32[8,2048]{1,0:T(8,128)S(1)} %fusion.80, f32[]{:T(128)} %bitcast.80, f32[]{:T(128)} %bitcast.79, ...), kind=kLoop, calls=%fused_computation.85 | loop fusion | flops 100352 | bytes 114800 | tf_op jit(solution)/shard_map/div | solution.py:30
  511.9 22.0 %subtract_divide_fusion = (f32[1,2048]{1,0:T(1,128)S(1)}, f32[1,2048]{1,0:T(1,128)S(1)}, f32[1,2048]{1,0:T(1,128)S(1)}, f32[1,2048]{1,0:T(1,128)S(1)}, f32[1,204...) fusion(f32[1,2048]{1,0:T(1,128)S(1)} %get-tuple-element.180, ...), kind=kLoop, calls=%fused_computation.77 | loop fusion | flops 159744 | bytes 131216 | tf_op jit(solution)/shard_map/div | solution.py:36
  533.9 0.1 stack.100
  534.0 0.2 fusion.50
  534.2 0.6 copy.27
  (26 shorter events, 0.3 us)
Async XLA Ops:
  23.4 27.9 %copy-start.3 = (s32[256]{0:T(256)S(1)}, s32[256]{0:T(256)}, u32[]{:S(2)}) copy-start(s32[256]{0:T(256)} %param.9) | copy-start | bytes 3076
  51.3 184.8 %copy-start.2 = (f32[1,2,1024]{2,1,0:T(2,128)S(1)}, f32[1,2,1024]{2,1,0:T(2,128)}, u32[]{:S(2)}) copy-start(f32[1,2,1024]{2,1,0:T(2,128)} %param.11) | copy-start | bytes 24580
  219.7 29.9 %all-to-all-start = ((bf16[128,2,512]{2,1,0:T(2,128)(2,1)}), bf16[128,2,512]{2,1,0:T(2,128)(2,1)S(1)}, u32[]{:S(2)}, u32[]{:S(2)}) async-start(bf16[128,2,512]{2,1,0:T(2,128)(2,1)} %convert_element_type.56), calls=%async_computation | async-start | bytes 524288 | tf_op jit(solution)/shard_map/all_to_all | solution.py:110
  236.0 254.5 %all-gather.2.cloned.1.call-start = ((), (), s32[]{:S(2)}) async-start(), calls=%async_computation.2 | async-start | bytes 2105344 | tf_op jit(solution)/shard_map/all_gather | solution.py:129
  260.2 93.0 %copy-start.1 = (s32[1024]{0:T(1024)S(1)}, s32[1024]{0:T(1024)}, u32[]{:S(2)}) copy-start(s32[1024]{0:T(1024)} %param.10) | copy-start | bytes 12292
  353.2 2.2 copy-start
Sparse Core Ops, SparseCore 0:
  391.8 98.7 all-gather.1
where the time goes:
time: 549 us; the launch traced here: 542 us
  matrix products  174 us (32%)
  waiting for transfers between devices  107 us (19%)
  other arithmetic  79 us (14%)
  blocking collectives  79 us (14%)
  local copies, waits for them, and re-layouts  42 us (8%)
  loops' own time  28.4 us (5%)
  starting transfers between devices  16.4 us (3%)
  between operations  15.8 us (3%)
    all_gather x1, waiting for transfers between devices, per_device(): everything = lax.all_gather(solved, ('grp', 'rep'), axis=0, tiled=True)  93.6 us
    psum x1, blocking collectives, per_device(): power = lax.psum(jnp.sum(autos, axis=0), ('grp', 'rep')) / kept  72.9 us
    dot_general x4, matrix products, transform_block(): jnp.einsum('kw,rw->kr', table_im, piece, preferred_element_type=jnp.float32)  69.5 us
    dot_general x4, matrix products, transform_block(): jnp.einsum('kw,rw->kr', table_re, piece, preferred_element_type=jnp.float32)  68.8 us
    another operation x1, loops' own time, per_device(): lax.fori_loop(0, nfft // width, transform_block, (empty, empty))  28.4 us
    convert_element_type x1, other arithmetic, per_device(): filtered = filtered.astype(jnp.bfloat16).reshape(inp_dev * spec, nfft)  27.9 us
    div x1, other arithmetic, solve_gram(): backward[row] = value / factor[row, row]  22 us
    div x1, other arithmetic, solve_gram(): forward.append(value / factor[row, row])  17.7 us
  transfers between devices with their start and end apart: 2, of which 2 were waited for; matrix products, arithmetic and copies ran while one was open for 1% of the time, Pallas kernels for 0%

commit v1 on v0

v1 whole, which is shorter than its diff:
```python
import math

import jax
import jax.numpy as jnp
from jax import lax
from jax.experimental import pallas as pl
from jax.experimental.pallas import tpu as pltpu
from jax.sharding import PartitionSpec as P

bf, f32 = jnp.bfloat16, jnp.float32
MESH = pl.DeviceIdType.MESH
CHAN = 8192
NFFT = 16384
SPEC = 64
TAPS = 4
FRAMES = SPEC + TAPS - 1
KEPT = 256
INPUTS = 1024
ITERS = 4
POLY = 8
NX, NY, NZ = 4, 4, 8
CHIPS = NX * NY * NZ
PLANE = NX * NY
TILES = NFFT // 128
QT = TILES // 4
CHUNKS = 8
KC = QT // CHUNKS


def turns(phase):
    quad = (phase + NFFT // 8) // (NFFT // 4)
    x = (phase - quad * (NFFT // 4)).astype(f32) * f32(2.0 * math.pi / NFFT)
    x2 = x * x
    s = x * (1.0 + x2 * (-1.0 / 6 + x2 * (1.0 / 120 + x2 * (-1.0 / 5040 + x2 * (1.0 / 362880)))))
    c = 1.0 + x2 * (-0.5 + x2 * (1.0 / 24 + x2 * (-1.0 / 720 + x2 * (1.0 / 40320))))
    odd = (quad & 1) == 1
    cc = jnp.where(odd, s, c)
    ss = jnp.where(odd, c, s)
    cc = jnp.where((quad == 1) | (quad == 2), -cc, cc)
    ss = jnp.where((quad == 2) | (quad == 3), -ss, ss)
    return cc, ss


def loop(f, n):
    def step(i, carry):
        f(i)
        return carry

    lax.fori_loop(0, n, step, 0)


def kernel(
    x_hbm, fir_ref, chan_ref, use_ref, gain_ref,
    solved_ref, band_ref,
    X, Fa, Fb, Ta, Tb, acc, hi, lo, wide, msgs, both, turned,
    pw, pz, pc, sol, splat, part, half, planes, fit, fit_out,
    in_sem, core_send, core_recv, own_sem, turn_send, turn_recv, self_sem,
    pw_send, pw_recv, pz_send, pz_recv, pc_send, pc_recv,
    sol_send, sol_recv, half_send, half_recv, z_send, z_recv, fit_send, fit_recv,
):
    g = lax.axis_index("grp")
    r = lax.axis_index("rep")
    z = lax.rem(g, NZ)
    xy = g // NZ
    y = lax.rem(xy, NY)
    x = xy // NY

    src = x_hbm.reshape(FRAMES, 4, QT, 4, 128)

    def sample_copy(k, j):
        at = pl.ds(KC * k, KC)
        return pltpu.make_async_copy(src.at[:, j, at], X.at[:, at, j], in_sem.at[k, j])

    for k in range(CHUNKS):
        for j in range(4):
            sample_copy(k, j).start()

    def chip_peer(i):
        k, m = i // PLANE, lax.rem(i, PLANE)
        sign = 1 - 2 * lax.rem(k, 2)
        dz = NZ // 2 + sign * ((k + 1) // 2)
        kx, ky = m // NY, lax.rem(m, NY)
        dx = NX // 2 + (1 - 2 * lax.rem(kx, 2)) * ((kx + 1) // 2)
        dy = NY // 2 + (1 - 2 * lax.rem(ky, 2)) * ((ky + 1) // 2)
        px, py, pz = lax.rem(x + dx, NX), lax.rem(y + dy, NY), lax.rem(z + dz, NZ)
        return (px * NY + py) * NZ + pz

    barrier = pltpu.get_barrier_semaphore()
    pl.semaphore_signal(barrier, inc=1, device_id=(g, 1 - r), device_id_type=MESH)
    loop(
        lambda i: pl.semaphore_signal(barrier, inc=1, device_id=(chip_peer(i), r), device_id_type=MESH),
        CHIPS - 1,
    )

    chan = chan_ref[...]

    def table(n0, rows, step):
        n = (lax.broadcasted_iota(jnp.int32, (rows, KEPT), 0) + n0) * step
        return turns((n * chan) & (NFFT - 1))

    c, s = table(0, QT, 128)
    hi[0] = c
    hi[1] = -s

    def low_table(i):
        c, s = table(i * 16, 16, 1)
        at = pl.ds(pl.multiple_of(i * 16, 16), 16)
        lo[0, at, :] = c
        lo[1, at, :] = -s

    loop(low_table, 8)

    rows = X.reshape(FRAMES, QT, 16, 128)
    quarter = lax.broadcasted_iota(jnp.int32, (16, 128), 0) // 4

    def fir(k, h, F, T):
        kk = KC * k + h
        static = isinstance(h, int)
        col = slice(h * 128, h * 128 + 128) if static else pl.ds(pl.multiple_of(h * 128, 128), 128)
        coef = []
        for t in range(TAPS):
            b = [jnp.broadcast_to(fir_ref[j * QT + kk, pl.ds(t, 1)], (16, 128)) for j in range(4)]
            coef.append(
                jnp.where(
                    quarter == 0, b[0], jnp.where(quarter == 1, b[1], jnp.where(quarter == 2, b[2], b[3]))
                )
            )
        w = [rows[f, kk].astype(f32) for f in range(TAPS - 1)]
        for s in range(SPEC):
            w.append(rows[s + TAPS - 1, kk].astype(f32))
            o = coef[0] * w[0] + coef[1] * w[1] + coef[2] * w[2] + coef[3] * w[3]
            F[s * 16 : (s + 1) * 16, col] = o.astype(bf)
            w = w[1:]
        hr, hm = hi[0, pl.ds(kk, 1), :], hi[1, pl.ds(kk, 1), :]
        for q in range(8):
            lr, lm = lo[0, q * 16 : (q + 1) * 16, :], lo[1, q * 16 : (q + 1) * 16, :]
            first = h * 128 + q * 16
            row = slice(first, first + 16) if static else pl.ds(pl.multiple_of(first, 16), 16)
            T[0, row, :] = (hr * lr - hm * lm).astype(bf)
            T[1, row, :] = (hr * lm + hm * lr).astype(bf)

    def mm(F, T):
        for n in range(2):
            d = jnp.dot(F[...], T[n], preferred_element_type=f32)
            for q in range(2):
                acc[2 * n + q] += d[:, q * 128 : (q + 1) * 128]

    def wait_samples(k):
        for j in range(4):
            sample_copy(k, j).wait()

    def stage(k, prev, cur):
        wait_samples(k)
        mm(*prev)
        for h in range(KC):
            fir(k, h, *cur)

    A, B = (Fa, Ta), (Fb, Tb)
    acc[...] = jnp.zeros_like(acc)
    wait_samples(0)
    loop(lambda h: fir(0, h, *A), KC)

    def pair(i):
        stage(2 * i + 1, A, B)
        stage(2 * i + 2, B, A)

    loop(pair, CHUNKS // 2 - 1)
    stage(CHUNKS - 1, A, B)
    mm(*B)

    quads = []
    for j in range(4):
        ph = (chan * j) & 3
        rr = jnp.where(ph == 0, 1.0, jnp.where(ph == 2, -1.0, 0.0))
        ri = jnp.where(ph == 1, -1.0, jnp.where(ph == 3, 1.0, 0.0))
        quads.append((rr, ri))
    sub8 = lax.broadcasted_iota(jnp.int32, (8, 128), 0)
    lane8 = lax.broadcasted_iota(jnp.int32, (8, 128), 1)
    power_row, power_lane = xy // 2, lax.rem(xy, 2) * 64 + z * 8 + r * 4
    powers = jnp.zeros((8, 128), f32)
    for p in range(4):
        sr = si = None
        for j in range(4):
            rr, ri = quads[j]
            at = pl.ds(j * 4 + p, SPEC, stride=16)
            a, b = [jnp.concatenate([acc[q, at, :], acc[q + 1, at, :]], axis=1) for q in (0, 2)]
            tr = rr * a - ri * b if j else a
            ti = rr * b + ri * a if j else b
            sr = tr if sr is None else sr + tr
            si = ti if si is None else si + ti
        v = jnp.concatenate([sr, si], axis=0)
        q = v.astype(bf).astype(f32)
        power = jnp.sum(jnp.sum(q * q, axis=1, keepdims=True), axis=0, keepdims=True)
        powers = jnp.where((sub8 == power_row) & (lane8 == power_lane + p), power, powers)
        wide[pl.ds(p, KEPT, stride=4), :] = v.T
    pw[xy] = powers * f32(1.0 / (SPEC * KEPT))
    pl.semaphore_wait(barrier, CHIPS)

    def send_plane(buf, send, recv):
        def one(i):
            t = lax.rem(xy + 1 + i, PLANE)
            pltpu.make_async_remote_copy(
                src_ref=buf.at[xy], dst_ref=buf.at[xy], send_sem=send, recv_sem=recv,
                device_id=(t * NZ + z, r), device_id_type=MESH,
            ).start()

        loop(one, PLANE - 1)

    def send_z(buf, send, recv):
        def one(i):
            t = lax.rem(z + 1 + i, NZ)
            pltpu.make_async_remote_copy(
                src_ref=buf.at[z], dst_ref=buf.at[z], send_sem=send, recv_sem=recv,
                device_id=(xy * NZ + t, r), device_id_type=MESH,
            ).start()

        loop(one, NZ - 1)

    def drain(buf, n, sem):
        pltpu.make_async_copy(buf.at[pl.ds(0, n)], buf.at[pl.ds(0, n)], sem).wait()

    send_plane(pw, pw_send, pw_recv)

    msgs.reshape(KEPT * 4, 128)[...] = wide[...].astype(bf)
    core_copy = pltpu.make_async_remote_copy(
        src_ref=msgs.at[1 - r], dst_ref=both.at[:, r], send_sem=core_send, recv_sem=core_recv,
        device_id=(g, 1 - r), device_id_type=MESH,
    )
    core_copy.start()
    own_copy = pltpu.make_async_copy(msgs.at[r], both.at[:, r], own_sem)
    own_copy.start()
    own_copy.wait()
    core_copy.wait_recv()

    def send_chip(i):
        t = chip_peer(i)
        pltpu.make_async_remote_copy(
            src_ref=both.at[t], dst_ref=turned.at[g], send_sem=turn_send, recv_sem=turn_recv,
            device_id=(t, r), device_id_type=MESH,
        ).start()

    loop(send_chip, CHIPS - 1)
    self_copy = pltpu.make_async_copy(both.at[g], turned.at[g], self_sem)
    self_copy.start()

    drain(pw, PLANE - 1, pw_recv)
    t = pw[0]
    for i in range(1, PLANE):
        t = t + pw[i]
    pz[z] = t
    send_z(pz, pz_send, pz_recv)

    u = chan.astype(f32) * f32(2.0 / (CHAN - 1)) - 1.0
    poly = [jnp.ones_like(u), u]
    for order in range(1, POLY - 1):
        poly.append(((2 * order + 1) * u * poly[order] - order * poly[order - 1]) / (order + 1))
    sub = lax.broadcasted_iota(jnp.int32, (POLY, KEPT), 0)
    basis = jnp.zeros((POLY, KEPT), f32)
    for k in range(POLY):
        basis = jnp.where(sub == k, jnp.broadcast_to(poly[k], (POLY, KEPT)), basis)
    lane = lax.broadcasted_iota(jnp.int32, (POLY, KEPT), 1)

    def column(q):
        return jnp.sum(jnp.where(lane == q, basis, 0.0), axis=1, keepdims=True)

    aug = jnp.zeros((POLY, 128), f32)
    for k in range(POLY):
        aug = jnp.where(lane8 == k, jnp.sum(basis * poly[k], axis=1, keepdims=True), aug)
    aug = jnp.where(lane8 == POLY, column(r * CHIPS + g), aug)
    aug = jnp.where(lane8 == POLY + 1, column((1 - r) * CHIPS + g), aug)
    for k in range(POLY):
        pivot_row = jnp.sum(jnp.where(sub8 == k, aug, 0.0), axis=0, keepdims=True)
        pivot = jnp.sum(jnp.where(lane8[0:1] == k, pivot_row, 0.0), axis=1, keepdims=True)
        pivot_row = pivot_row / pivot
        factor = jnp.sum(jnp.where(lane8 == k, aug, 0.0), axis=1, keepdims=True)
        aug = jnp.where(sub8 == k, pivot_row, aug - factor * pivot_row)
    for i in range(2):
        v = jnp.sum(jnp.where(lane8 == POLY + i, aug, 0.0), axis=1, keepdims=True)
        splat[PLANE + i] = jnp.broadcast_to(v, (POLY, 128))
    for i in range(PLANE):
        splat[i] = jnp.broadcast_to(column(r * CHIPS + i * NZ + z), (POLY, 128))

    drain(pz, NZ - 1, pz_recv)
    t = pz[0]
    for i in range(1, NZ):
        t = t + pz[i]
    pc[r] = t
    power_copy = pltpu.make_async_remote_copy(
        src_ref=pc.at[r], dst_ref=pc.at[r], send_sem=pc_send, recv_sem=pc_recv,
        device_id=(g, 1 - r), device_id_type=MESH,
    )
    power_copy.start()
    power_copy.wait_recv()
    t = lax.rsqrt(pc[0] + pc[1] + f32(1e-06))
    scale = jnp.concatenate([t[j : j + 1, :] for j in range(8)], axis=1)

    self_copy.wait()
    drain(turned, CHIPS - 1, turn_recv)

    eye = (
        lax.broadcasted_iota(jnp.int32, (128, 128), 0) == lax.broadcasted_iota(jnp.int32, (128, 128), 1)
    ).astype(f32).astype(bf)
    cols = lax.dot_general(
        eye, turned.reshape(INPUTS, 128)[...], (((1,), (1,)), ((), ())), preferred_element_type=f32
    )
    xr, xi = cols[0:SPEC], cols[SPEC : 2 * SPEC]
    use = use_ref[...].astype(f32)
    scale = scale * use
    gr, gi = gain_ref[0:1, :], gain_ref[1:2, :]
    for step in range(ITERS):
        ar, ai = gr * scale, gi * scale
        zr = xr * ar - xi * ai
        zi = xr * ai + xi * ar
        dr = jnp.sum(zr, axis=1, keepdims=True) - zr
        di = jnp.sum(zi, axis=1, keepdims=True) - zi
        nr = jnp.sum(xr * dr + xi * di, axis=0, keepdims=True) * f32(1.0 / SPEC) * scale
        ni = jnp.sum(xr * di - xi * dr, axis=0, keepdims=True) * f32(1.0 / SPEC) * scale
        mag = use * (gr * gr + gi * gi)
        denom = jnp.sum(mag, axis=1, keepdims=True) - mag + f32(1e-06)
        fr, fi = nr / denom, ni / denom
        if step % 2 == 1:
            gr, gi = (fr + gr) * 0.5, (fi + gi) * 0.5
        else:
            gr, gi = fr, fi
    solved_ref[0:1, :] = gr
    solved_ref[1:2, :] = gi
    packed = []
    for v in (gr, gi):
        t = jnp.zeros((8, 128), f32)
        for j in range(8):
            t = jnp.where(sub8 == j, jnp.broadcast_to(v[:, j * 128 : (j + 1) * 128], (8, 128)), t)
        packed.append(t)
    sol[xy] = jnp.concatenate(packed, axis=0)

    send_plane(sol, sol_send, sol_recv)
    drain(sol, PLANE - 1, sol_recv)
    for k in range(POLY):
        m = None
        for i in range(PLANE):
            t = sol[i] * splat[i, k : k + 1, :]
            m = t if m is None else m + t
        part[0, k] = m[0:8]
        part[1, k] = m[8:16]
    half_copy = pltpu.make_async_remote_copy(
        src_ref=part.at[1 - r], dst_ref=half, send_sem=half_send, recv_sem=half_recv,
        device_id=(g, 1 - r), device_id_type=MESH,
    )
    half_copy.start()
    half_copy.wait_recv()
    planes[z] = part[r] + half[...]

    send_z(planes, z_send, z_recv)
    drain(planes, NZ - 1, z_recv)
    mine = theirs = None
    for k in range(POLY):
        m = planes[0, k]
        for i in range(1, NZ):
            m = m + planes[i, k]
        a, b = m * splat[PLANE, k : k + 1, :], m * splat[PLANE + 1, k : k + 1, :]
        mine = a if mine is None else mine + a
        theirs = b if theirs is None else theirs + b
    fit_out[...] = theirs
    fit_copy = pltpu.make_async_remote_copy(
        src_ref=fit_out, dst_ref=fit.at[r], send_sem=fit_send, recv_sem=fit_recv,
        device_id=(g, 1 - r), device_id_type=MESH,
    )
    fit_copy.start()
    fit[r] = mine
    fit_copy.wait_recv()
    for i in range(2):
        for j in range(8):
            band_ref[i : i + 1, j * 128 : (j + 1) * 128] = fit[i, j : j + 1, :]

    core_copy.wait_send()
    drain(both, CHIPS - 1, turn_send)
    drain(pw, PLANE - 1, pw_send)
    drain(pz, NZ - 1, pz_send)
    power_copy.wait_send()
    drain(sol, PLANE - 1, sol_send)
    half_copy.wait_send()
    drain(planes, NZ - 1, z_send)
    fit_copy.wait_send()


def per_device(samples, fir_coeffs, kept_channels, usable, initial_gains):
    tiles = samples.reshape(4, FRAMES * TILES, 128).transpose(1, 0, 2)
    coeffs = fir_coeffs.reshape(TAPS, TILES, 128).transpose(1, 0, 2)
    chan = kept_channels.reshape(CHIPS, 2).T.reshape(1, KEPT)
    vmem = pl.BlockSpec(memory_space=pltpu.VMEM)
    dma = pltpu.SemaphoreType.DMA
    solved, band = pl.pallas_call(
        kernel,
        name="fx_calibrate",
        out_shape=[jax.ShapeDtypeStruct((2, INPUTS), f32)] * 2,
        in_specs=[pl.BlockSpec(memory_space=pl.ANY)] + [vmem] * 4,
        out_specs=[vmem] * 2,
        scratch_shapes=[
            pltpu.VMEM((FRAMES, QT, 4, 4, 128), bf),
            pltpu.VMEM((16 * SPEC, KC * 128), bf),
            pltpu.VMEM((16 * SPEC, KC * 128), bf),
            pltpu.VMEM((2, KC * 128, KEPT), bf),
            pltpu.VMEM((2, KC * 128, KEPT), bf),
            pltpu.VMEM((4, 16 * SPEC, 128), f32),
            pltpu.VMEM((2, QT, KEPT), f32),
            pltpu.VMEM((2, 128, KEPT), f32),
            pltpu.VMEM((4 * KEPT, 128), f32),
            pltpu.VMEM((2, CHIPS, 4, 128), bf),
            pltpu.VMEM((CHIPS, 2, 4, 128), bf),
            pltpu.VMEM((CHIPS, 2, 4, 128), bf),
            pltpu.VMEM((PLANE, 8, 128), f32),
            pltpu.VMEM((NZ, 8, 128), f32),
            pltpu.VMEM((2, 8, 128), f32),
            pltpu.VMEM((PLANE, 16, 128), f32),
            pltpu.VMEM((PLANE + 2, POLY, 128), f32),
            pltpu.VMEM((2, POLY, 8, 128), f32),
            pltpu.VMEM((POLY, 8, 128), f32),
            pltpu.VMEM((NZ, POLY, 8, 128), f32),
            pltpu.VMEM((2, 8, 128), f32),
            pltpu.VMEM((8, 128), f32),
            dma((CHUNKS, 4)),
        ]
        + [dma] * 20,
        compiler_params=pltpu.CompilerParams(
            collective_id=0, has_side_effects=True, vmem_limit_bytes=48 * 2**20
        ),
    )(tiles, coeffs, chan, usable.reshape(1, INPUTS), initial_gains.reshape(2, INPUTS))
    return solved.reshape(1, 2, INPUTS), band.reshape(1, 2, INPUTS)


def solution(mesh):
    placed = (P(("grp", "rep"), None), P(), P(), P(), P(("grp", "rep"), None, None))
    return jax.shard_map(
        per_device,
        mesh=mesh,
        in_specs=placed,
        out_specs=(P(("grp", "rep"), None, None), P(("grp", "rep"), None, None)),
        check_vma=False,
    )
```

time: 549 us -> 59.1 us (0.11); the launches traced: 542 us -> 58.9 us
  matrix products: 174 us -> 0 us
  waiting for transfers between devices: 107 us -> 0 us
  other arithmetic: 79 us -> 0 us
  blocking collectives: 79 us -> 0 us
  Pallas kernels: 0 us -> 53.8 us
  local copies, waits for them, and re-layouts: 42 us -> 4.43 us
  loops' own time: 28.4 us -> 0 us
  starting transfers between devices: 16.4 us -> 0 us
  between operations: 15.8 us -> 0.65 us
    dot_general x21 -> x0, matrix products: 174 us -> none  [the longest x4 69.5 us: transform_block(): jnp.einsum('kw,rw->kr', table_im, piece, preferred_element_type=jnp.float32)]
    all_gather x1 -> x0, waiting for transfers between devices: 93.6 us -> none  [per_device(): everything = lax.all_gather(solved, ('grp', 'rep'), axis=0, tiled=True)]
    psum x1 -> x0, blocking collectives: 72.9 us -> none  [per_device(): power = lax.psum(jnp.sum(autos, axis=0), ('grp', 'rep')) / kept]
    pallas_call x0 -> x1, Pallas kernels: none -> 53.8 us  [per_device(): pl.pallas_call(kernel, name='fx_calibrate', out_shape=[jax.ShapeDtypeStru...]
    div x6 -> x0, other arithmetic: 40.5 us -> none  [the longest x1 22 us: solve_gram(): backward[row] = value / factor[row, row]]
    another operation x1 -> x0, loops' own time: 28.4 us -> none  [per_device(): lax.fori_loop(0, nfft // width, transform_block, (empty, empty))]
    convert_element_type x1 -> x0, other arithmetic: 27.9 us -> none  [per_device(): filtered = filtered.astype(jnp.bfloat16).reshape(inp_dev * spec, nfft)]
    gather x1 -> x0, local copies, waits for them, and re-layouts: 17.3 us -> none  [per_device(): autos = jnp.diagonal(vis_re, axis1=1, axis2=2)]
  transfers between devices with their start and end apart: 2 -> 0, of which waited for: 2 -> 0; matrix products, arithmetic and copies ran while one was open for 1% -> 0% of each run, Pallas kernels for 0% -> 0%
where the time goes in v1:
time: 59.1 us; the launch traced here: 58.9 us
  Pallas kernels  53.8 us (91%)
  local copies, waits for them, and re-layouts  4.43 us (7%)
  between operations  0.65 us (1%)
    pallas_call x1, Pallas kernels, per_device(): pl.pallas_call(kernel, name='fx_calibrate', out_shape=[jax.ShapeDtypeStru...  53.8 us
    unnamed x8, local copies, waits for them, and re-layouts  3.55 us

profile of v1, /device:TPU:1, one launch (start us, length us, event | category | flops | bytes accessed | tf_op | source)
XLA Modules:
  0.0 58.9 jit_solution(1009800779449272488)
XLA Ops:
  0.6 0.8 %reshape.30 = s32[128,2]{1,0:T(8,128)S(1)} reshape(s32[256]{0:T(256)} %param.7) | data formatting | bytes 2048 | tf_op jit(solution)/shard_map/reshape | solution.py:388
  1.4 0.1 copy.7
  1.5 0.0 copy-start
  1.5 1.0 %copy-done = f32[4,16384]{1,0:T(4,128)S(1)} copy-done((f32[4,16384]{1,0:T(4,128)S(1)}, f32[4,16384]{1,0:T(4,128)}, u32[]{:S(2)}) %copy-start) | copy-done | bytes 262168
  2.5 0.0 copy-start.1
  2.5 0.7 %copy-done.1 = f32[1,2,1024]{2,1,0:T(2,128)S(1)} copy-done((f32[1,2,1024]{2,1,0:T(2,128)S(1)}, f32[1,2,1024]{2,1,0:T(2,128)}, u32[]{:S(2)}) %copy-start.1) | copy-done | bytes 8216
  3.2 0.0 copy-start.2
  3.2 0.7 %copy-done.2 = s32[1024]{0:T(1024)S(1)} copy-done((s32[1024]{0:T(1024)S(1)}, s32[1024]{0:T(1024)}, u32[]{:S(2)}) %copy-start.2) | copy-done | bytes 4120
  3.9 53.8 %fx_calibrate.1 = (f32[2,1024]{1,0:T(2,128)S(1)}, f32[2,1024]{1,0:T(2,128)S(1)}) custom-call(bf16[8576,4,128]{2,1,0:T(4,128)(2,1)} %bitcast.18, f32[128,4,128]{2,1,0:T(4,128)S(1)} %bitcast.12, s32[1,256]{1,0:T(1,128)S(1)} %bitcast.17, s32[1,1024]{1,0:T(1,128)S(1)} %bitcast.16, f32[2,1024]{1,0:T(2,128)S(1)} %bitcast.13), custom_call_target="tpu_custom_call" | custom-call | tf_op jit(solution)/shard_map/fx_calibrate/pallas_call | solution.py:391
  57.7 0.6 %copy.10 = f32[1,2,1024]{2,1,0:T(2,128)} copy(f32[1,2,1024]{2,1,0:T(2,128)S(1)} %bitcast.15) | data formatting | bytes 16384
  58.3 0.6 %copy.11 = f32[1,2,1024]{2,1,0:T(2,128)} copy(f32[1,2,1024]{2,1,0:T(2,128)S(1)} %bitcast.14) | data formatting | bytes 16384
Async XLA Ops:
  1.5 1.0 %copy-start = (f32[4,16384]{1,0:T(4,128)S(1)}, f32[4,16384]{1,0:T(4,128)}, u32[]{:S(2)}) copy-start(f32[4,16384]{1,0:T(4,128)} %param.6) | copy-start | bytes 786436
  2.5 0.7 %copy-start.1 = (f32[1,2,1024]{2,1,0:T(2,128)S(1)}, f32[1,2,1024]{2,1,0:T(2,128)}, u32[]{:S(2)}) copy-start(f32[1,2,1024]{2,1,0:T(2,128)} %param.9) | copy-start | bytes 24580
  3.2 0.7 %copy-start.2 = (s32[1024]{0:T(1024)S(1)}, s32[1024]{0:T(1024)}, u32[]{:S(2)}) copy-start(s32[1024]{0:T(1024)} %param.8) | copy-start | bytes 12292

commit v2 on v1

--- a/solution.py
+++ b/solution.py
@@ -50,13 +50,14 @@
 
 
 def kernel(
-    x_hbm, fir_ref, chan_ref, use_ref, gain_ref,
+    x_hbm, fir_hbm, chan_hbm, use_hbm, gain_hbm,
     solved_ref, band_ref,
-    X, Fa, Fb, Ta, Tb, acc, hi, lo, wide, msgs, both, turned,
-    pw, pz, pc, sol, splat, part, half, planes, fit, fit_out,
-    in_sem, core_send, core_recv, own_sem, turn_send, turn_recv, self_sem,
-    pw_send, pw_recv, pz_send, pz_recv, pc_send, pc_recv,
-    sol_send, sol_recv, half_send, half_recv, z_send, z_recv, fit_send, fit_recv,
+    X, fir_ref, chan_ref, use_ref, gain_ref,
+    Fa, Fb, Ta, Tb, acc, hi, lo, wide, msgs, both, turned,
+    pw, pz, mysol, sol, splat, planes, fit, fit_out,
+    in_sem, arg_sem, core_send, core_recv, own_sem, turn_send, turn_recv, self_sem,
+    pw_send, pw_recv, pz_send, pz_recv,
+    sol_send, sol_recv, z_send, z_recv, fit_send, fit_recv, ready,
 ):
     g = lax.axis_index("grp")
     r = lax.axis_index("rep")
@@ -71,27 +72,42 @@
         at = pl.ds(KC * k, KC)
         return pltpu.make_async_copy(src.at[:, j, at], X.at[:, at, j], in_sem.at[k, j])
 
+    args = [
+        pltpu.make_async_copy(a, b, arg_sem.at[i])
+        for i, (a, b) in enumerate(
+            [(chan_hbm, chan_ref), (fir_hbm, fir_ref), (use_hbm, use_ref), (gain_hbm, gain_ref)]
+        )
+    ]
+    args[0].start()
+    args[1].start()
     for k in range(CHUNKS):
         for j in range(4):
             sample_copy(k, j).start()
-
-    def chip_peer(i):
-        k, m = i // PLANE, lax.rem(i, PLANE)
-        sign = 1 - 2 * lax.rem(k, 2)
-        dz = NZ // 2 + sign * ((k + 1) // 2)
-        kx, ky = m // NY, lax.rem(m, NY)
-        dx = NX // 2 + (1 - 2 * lax.rem(kx, 2)) * ((kx + 1) // 2)
-        dy = NY // 2 + (1 - 2 * lax.rem(ky, 2)) * ((ky + 1) // 2)
-        px, py, pz = lax.rem(x + dx, NX), lax.rem(y + dy, NY), lax.rem(z + dz, NZ)
-        return (px * NY + py) * NZ + pz
+    args[2].start()
+    args[3].start()
 
     barrier = pltpu.get_barrier_semaphore()
-    pl.semaphore_signal(barrier, inc=1, device_id=(g, 1 - r), device_id_type=MESH)
-    loop(
-        lambda i: pl.semaphore_signal(barrier, inc=1, device_id=(chip_peer(i), r), device_id_type=MESH),
-        CHIPS - 1,
-    )
-
+
+    def greet(chip, core):
+        pl.semaphore_signal(barrier, inc=1, device_id=(chip, core), device_id_type=MESH)
+
+    def greet_plane(i):
+        t = lax.rem(xy * 2 + r + 1 + i, 2 * PLANE)
+        greet(t // 2 * NZ + z, lax.rem(t, 2))
+
+    loop(greet_plane, 2 * PLANE - 1)
+    loop(lambda i: greet(xy * NZ + lax.rem(z + 1 + i, NZ), r), NZ - 1)
+
+    def plane_is_here():
+        pl.semaphore_wait(barrier, 2 * PLANE - 1 + NZ - 1)
+        loop(
+            lambda i: pl.semaphore_signal(
+                ready, inc=1, device_id=(xy * NZ + lax.rem(z + 1 + i, NZ), r), device_id_type=MESH
+            ),
+            NZ - 1,
+        )
+
+    args[0].wait()
     chan = chan_ref[...]
 
     def table(n0, rows, step):
@@ -157,10 +173,12 @@
 
     A, B = (Fa, Ta), (Fb, Tb)
     acc[...] = jnp.zeros_like(acc)
+    args[1].wait()
     wait_samples(0)
     loop(lambda h: fir(0, h, *A), KC)
 
     def pair(i):
+        pl.when(i == CHUNKS // 2 - 2)(plane_is_here)
         stage(2 * i + 1, A, B)
         stage(2 * i + 2, B, A)
 
@@ -178,6 +196,7 @@
     lane8 = lax.broadcasted_iota(jnp.int32, (8, 128), 1)
     power_row, power_lane = xy // 2, lax.rem(xy, 2) * 64 + z * 8 + r * 4
     powers = jnp.zeros((8, 128), f32)
+    spectra = []
     for p in range(4):
         sr = si = None
         for j in range(4):
@@ -192,19 +211,20 @@
         q = v.astype(bf).astype(f32)
         power = jnp.sum(jnp.sum(q * q, axis=1, keepdims=True), axis=0, keepdims=True)
         powers = jnp.where((sub8 == power_row) & (lane8 == power_lane + p), power, powers)
-        wide[pl.ds(p, KEPT, stride=4), :] = v.T
-    pw[xy] = powers * f32(1.0 / (SPEC * KEPT))
-    pl.semaphore_wait(barrier, CHIPS)
-
-    def send_plane(buf, send, recv):
+        spectra.append(v)
+    pw[xy * 2 + r] = powers * f32(1.0 / (SPEC * KEPT))
+    pl.semaphore_wait(ready, NZ - 1)
+
+    def send_plane(source, buf, send, recv):
         def one(i):
-            t = lax.rem(xy + 1 + i, PLANE)
+            t = lax.rem(xy * 2 + r + 1 + i, 2 * PLANE)
+            core = lax.rem(t, 2)
             pltpu.make_async_remote_copy(
-                src_ref=buf.at[xy], dst_ref=buf.at[xy], send_sem=send, recv_sem=recv,
-                device_id=(t * NZ + z, r), device_id_type=MESH,
+                src_ref=source(core), dst_ref=buf.at[xy * 2 + r], send_sem=send, recv_sem=recv,
+                device_id=(t // 2 * NZ + z, core), device_id_type=MESH,
             ).start()
 
-        loop(one, PLANE - 1)
+        loop(one, 2 * PLANE - 1)
 
     def send_z(buf, send, recv):
         def one(i):
@@ -219,33 +239,41 @@
     def drain(buf, n, sem):
         pltpu.make_async_copy(buf.at[pl.ds(0, n)], buf.at[pl.ds(0, n)], sem).wait()
 
-    send_plane(pw, pw_send, pw_recv)
-
+    send_plane(lambda core: pw.at[xy * 2 + r], pw, pw_send, pw_recv)
+
+    for p in range(4):
+        wide[pl.ds(p, KEPT, stride=4), :] = spectra[p].T
     msgs.reshape(KEPT * 4, 128)[...] = wide[...].astype(bf)
     core_copy = pltpu.make_async_remote_copy(
-        src_ref=msgs.at[1 - r], dst_ref=both.at[:, r], send_sem=core_send, recv_sem=core_recv,
+        src_ref=msgs.at[:, 1 - r], dst_ref=both.at[:, r], send_sem=core_send, recv_sem=core_recv,
         device_id=(g, 1 - r), device_id_type=MESH,
     )
     core_copy.start()
-    own_copy = pltpu.make_async_copy(msgs.at[r], both.at[:, r], own_sem)
+    own_copy = pltpu.make_async_copy(msgs.at[:, r], both.at[:, r], own_sem)
     own_copy.start()
     own_copy.wait()
     core_copy.wait_recv()
 
-    def send_chip(i):
-        t = chip_peer(i)
+    def send_chip(t):
         pltpu.make_async_remote_copy(
             src_ref=both.at[t], dst_ref=turned.at[g], send_sem=turn_send, recv_sem=turn_recv,
             device_id=(t, r), device_id_type=MESH,
         ).start()
 
-    loop(send_chip, CHIPS - 1)
+    def send_level(k):
+        pz_ = lax.rem(z + NZ // 2 + (1 - 2 * lax.rem(k, 2)) * ((k + 1) // 2), NZ)
+        for m in range(PLANE):
+            send_chip(lax.rem(xy + PLANE // 2 + m, PLANE) * NZ + pz_)
+
+    loop(send_level, NZ - 1)
+    for m in range(1, PLANE):
+        send_chip(lax.rem(xy + m, PLANE) * NZ + z)
     self_copy = pltpu.make_async_copy(both.at[g], turned.at[g], self_sem)
     self_copy.start()
 
-    drain(pw, PLANE - 1, pw_recv)
+    drain(pw, 2 * PLANE - 1, pw_recv)
     t = pw[0]
-    for i in range(1, PLANE):
+    for i in range(1, 2 * PLANE):
         t = t + pw[i]
     pz[z] = t
     send_z(pz, pz_send, pz_recv)
@@ -266,8 +294,8 @@
     aug = jnp.zeros((POLY, 128), f32)
     for k in range(POLY):
         aug = jnp.where(lane8 == k, jnp.sum(basis * poly[k], axis=1, keepdims=True), aug)
-    aug = jnp.where(lane8 == POLY, column(r * CHIPS + g), aug)
-    aug = jnp.where(lane8 == POLY + 1, column((1 - r) * CHIPS + g), aug)
+    aug = jnp.where(lane8 == POLY, column(2 * g + r), aug)
+    aug = jnp.where(lane8 == POLY + 1, column(2 * g + 1 - r), aug)
     for k in range(POLY):
         pivot_row = jnp.sum(jnp.where(sub8 == k, aug, 0.0), axis=0, keepdims=True)
         pivot = jnp.sum(jnp.where(lane8[0:1] == k, pivot_row, 0.0), axis=1, keepdims=True)
@@ -276,24 +304,19 @@
         aug = jnp.where(sub8 == k, pivot_row, aug - factor * pivot_row)
     for i in range(2):
         v = jnp.sum(jnp.where(lane8 == POLY + i, aug, 0.0), axis=1, keepdims=True)
-        splat[PLANE + i] = jnp.broadcast_to(v, (POLY, 128))
-    for i in range(PLANE):
-        splat[i] = jnp.broadcast_to(column(r * CHIPS + i * NZ + z), (POLY, 128))
+        splat[2 * PLANE + i] = jnp.broadcast_to(v, (POLY, 128))
+    for i in range(2 * PLANE):
+        splat[i] = jnp.broadcast_to(column(i // 2 * (2 * NZ) + z * 2 + i % 2), (POLY, 128))
 
     drain(pz, NZ - 1, pz_recv)
     t = pz[0]
     for i in range(1, NZ):
         t = t + pz[i]
-    pc[r] = t
-    power_copy = pltpu.make_async_remote_copy(
-        src_ref=pc.at[r], dst_ref=pc.at[r], send_sem=pc_send, recv_sem=pc_recv,
-        device_id=(g, 1 - r), device_id_type=MESH,
-    )
-    power_copy.start()
-    power_copy.wait_recv()
-    t = lax.rsqrt(pc[0] + pc[1] + f32(1e-06))
+    t = lax.rsqrt(t + f32(1e-06))
     scale = jnp.concatenate([t[j : j + 1, :] for j in range(8)], axis=1)
 
+    args[2].wait()
+    args[3].wait()
     self_copy.wait()
     drain(turned, CHIPS - 1, turn_recv)
 
@@ -324,39 +347,34 @@
             gr, gi = fr, fi
     solved_ref[0:1, :] = gr
     solved_ref[1:2, :] = gi
-    packed = []
-    for v in (gr, gi):
+    for i, v in enumerate((gr, gi)):
         t = jnp.zeros((8, 128), f32)
         for j in range(8):
             t = jnp.where(sub8 == j, jnp.broadcast_to(v[:, j * 128 : (j + 1) * 128], (8, 128)), t)
-        packed.append(t)
-    sol[xy] = jnp.concatenate(packed, axis=0)
-
-    send_plane(sol, sol_send, sol_recv)
-    drain(sol, PLANE - 1, sol_recv)
+        mysol[i] = t
+
+    send_plane(lambda core: mysol.at[core], sol, sol_send, sol_recv)
+    sol[xy * 2 + r] = mysol[r]
+    drain(sol, 2 * PLANE - 1, sol_recv)
+    part = []
     for k in range(POLY):
         m = None
-        for i in range(PLANE):
+        for i in range(2 * PLANE):
             t = sol[i] * splat[i, k : k + 1, :]
             m = t if m is None else m + t
-        part[0, k] = m[0:8]
-        part[1, k] = m[8:16]
-    half_copy = pltpu.make_async_remote_copy(
-        src_ref=part.at[1 - r], dst_ref=half, send_sem=half_send, recv_sem=half_recv,
-        device_id=(g, 1 - r), device_id_type=MESH,
-    )
-    half_copy.start()
-    half_copy.wait_recv()
-    planes[z] = part[r] + half[...]
-
+        part.append(m)
+    part = jnp.concatenate(part, axis=0)
+    sent = part.astype(bf)
+    planes[z] = sent
     send_z(planes, z_send, z_recv)
+    total = part - sent.astype(f32)
     drain(planes, NZ - 1, z_recv)
+    for i in range(NZ):
+        total = total + planes[i].astype(f32)
     mine = theirs = None
     for k in range(POLY):
-        m = planes[0, k]
-        for i in range(1, NZ):
-            m = m + planes[i, k]
-        a, b = m * splat[PLANE, k : k + 1, :], m * splat[PLANE + 1, k : k + 1, :]
+        m = total[8 * k : 8 * (k + 1)]
+        a, b = m * splat[2 * PLANE, k : k + 1, :], m * splat[2 * PLANE + 1, k : k + 1, :]
         mine = a if mine is None else mine + a
         theirs = b if theirs is None else theirs + b
     fit_out[...] = theirs
@@ -373,11 +391,9 @@
 
     core_copy.wait_send()
     drain(both, CHIPS - 1, turn_send)
-    drain(pw, PLANE - 1, pw_send)
+    drain(pw, 2 * PLANE - 1, pw_send)
     drain(pz, NZ - 1, pz_send)
-    power_copy.wait_send()
-    drain(sol, PLANE - 1, sol_send)
-    half_copy.wait_send()
+    drain(sol, 2 * PLANE - 1, sol_send)
     drain(planes, NZ - 1, z_send)
     fit_copy.wait_send()
 
@@ -385,17 +401,21 @@
 def per_device(samples, fir_coeffs, kept_channels, usable, initial_gains):
     tiles = samples.reshape(4, FRAMES * TILES, 128).transpose(1, 0, 2)
     coeffs = fir_coeffs.reshape(TAPS, TILES, 128).transpose(1, 0, 2)
-    chan = kept_channels.reshape(CHIPS, 2).T.reshape(1, KEPT)
+    chan = kept_channels.reshape(1, KEPT)
     vmem = pl.BlockSpec(memory_space=pltpu.VMEM)
     dma = pltpu.SemaphoreType.DMA
     solved, band = pl.pallas_call(
         kernel,
         name="fx_calibrate",
         out_shape=[jax.ShapeDtypeStruct((2, INPUTS), f32)] * 2,
-        in_specs=[pl.BlockSpec(memory_space=pl.ANY)] + [vmem] * 4,
+        in_specs=[pl.BlockSpec(memory_space=pltpu.HBM)] * 5,
         out_specs=[vmem] * 2,
         scratch_shapes=[
             pltpu.VMEM((FRAMES, QT, 4, 4, 128), bf),
+            pltpu.VMEM((TILES, TAPS, 128), f32),
+            pltpu.VMEM((1, KEPT), jnp.int32),
+            pltpu.VMEM((1, INPUTS), jnp.int32),
+            pltpu.VMEM((2, INPUTS), f32),
             pltpu.VMEM((16 * SPEC, KC * 128), bf),
             pltpu.VMEM((16 * SPEC, KC * 128), bf),
             pltpu.VMEM((2, KC * 128, KEPT), bf),
@@ -404,24 +424,24 @@
             pltpu.VMEM((2, QT, KEPT), f32),
             pltpu.VMEM((2, 128, KEPT), f32),
             pltpu.VMEM((4 * KEPT, 128), f32),
-            pltpu.VMEM((2, CHIPS, 4, 128), bf),
             pltpu.VMEM((CHIPS, 2, 4, 128), bf),
             pltpu.VMEM((CHIPS, 2, 4, 128), bf),
-            pltpu.VMEM((PLANE, 8, 128), f32),
+            pltpu.VMEM((CHIPS, 2, 4, 128), bf),
+            pltpu.VMEM((2 * PLANE, 8, 128), f32),
             pltpu.VMEM((NZ, 8, 128), f32),
             pltpu.VMEM((2, 8, 128), f32),
-            pltpu.VMEM((PLANE, 16, 128), f32),
-            pltpu.VMEM((PLANE + 2, POLY, 128), f32),
-            pltpu.VMEM((2, POLY, 8, 128), f32),
-            pltpu.VMEM((POLY, 8, 128), f32),
-            pltpu.VMEM((NZ, POLY, 8, 128), f32),
+            pltpu.VMEM((2 * PLANE, 8, 128), f32),
+            pltpu.VMEM((2 * PLANE + 2, POLY, 128), f32),
+            pltpu.VMEM((NZ, POLY * 8, 128), bf),
             pltpu.VMEM((2, 8, 128), f32),
             pltpu.VMEM((8, 128), f32),
             dma((CHUNKS, 4)),
+            dma((4,)),
         ]
-        + [dma] * 20,
+        + [dma] * 16
+        + [pltpu.SemaphoreType.REGULAR],
         compiler_params=pltpu.CompilerParams(
-            collective_id=0, has_side_effects=True, vmem_limit_bytes=48 * 2**20
+            collective_id=0, has_side_effects=True, vmem_limit_bytes=60 * 2**20
         ),
     )(tiles, coeffs, chan, usable.reshape(1, INPUTS), initial_gains.reshape(2, INPUTS))
     return solved.reshape(1, 2, INPUTS), band.reshape(1, 2, INPUTS)

time: 59.1 us -> 48.7 us (0.82)
  Pallas kernels: 53.8 us -> 45.2 us
  local copies, waits for them, and re-layouts: 4.43 us -> 2.59 us
    pallas_call x1, Pallas kernels: 53.8 us -> 45.2 us  [per_device(): pl.pallas_call(kernel, name='fx_calibrate', out_shape=[jax.ShapeDtypeStru...]
    unnamed x8 -> x2, local copies, waits for them, and re-layouts: 3.55 us -> 2.59 us
    reshape x1 -> x0, local copies, waits for them, and re-layouts: 0.81 us -> none  [per_device(): chan = kept_channels.reshape(CHIPS, 2).T.reshape(1, KEPT)]
where the time goes in v2:
time: 48.7 us; the launch traced here: 48.5 us
  Pallas kernels  45.2 us (93%)
  local copies, waits for them, and re-layouts  2.59 us (5%)
  between operations  0.64 us (1%)
    pallas_call x1, Pallas kernels, per_device(): pl.pallas_call(kernel, name='fx_calibrate', out_shape=[jax.ShapeDtypeStru...  45.2 us
    unnamed x2, local copies, waits for them, and re-layouts  2.59 us

profile of v2, /device:TPU:1, one launch (start us, length us, event | category | flops | bytes accessed | tf_op | source)
XLA Modules:
  0.0 48.5 jit_solution(15881031953735786587)
XLA Ops:
  0.6 45.2 %fx_calibrate.1 = (f32[2,1024]{1,0:T(2,128)}, f32[2,1024]{1,0:T(2,128)}) custom-call(bf16[8576,4,128]{2,1,0:T(4,128)(2,1)} %bitcast.11, f32[128,4,128]{2,1,0:T(4,128)} %bitcast.12, s32[1,256]{1,0:T(1,128)} %bitcast.17, s32[1,1024]{1,0:T(1,128)} %bitcast.16, f32[2,1024]{1,0:T(2,128)} %bitcast.13), custom_call_target="tpu_custom_call" | custom-call | tf_op jit(solution)/shard_map/fx_calibrate/pallas_call | solution.py:407
  45.9 1.3 %copy.9 = f32[1,2,1024]{2,1,0:T(2,128)} copy(f32[1,2,1024]{2,1,0:T(2,128)} %bitcast.15) | data formatting | bytes 16384
  47.2 1.3 %copy.10 = f32[1,2,1024]{2,1,0:T(2,128)} copy(f32[1,2,1024]{2,1,0:T(2,128)} %bitcast.14) | data formatting | bytes 16384

commit v3 on v2

--- a/solution.py
+++ b/solution.py
@@ -41,6 +41,16 @@
     return cc, ss
 
 
+def far_first(n):
+    return sorted(range(n), key=lambda d: -min(d, n - d))
+
+
+PLANE_ORDER = sorted(
+    ((dx, dy) for dx in range(NX) for dy in range(NY)),
+    key=lambda d: -min(d[0], NX - d[0]) - min(d[1], NY - d[1]),
+)
+
+
 def loop(f, n):
     def step(i, carry):
         f(i)
@@ -53,9 +63,9 @@
     x_hbm, fir_hbm, chan_hbm, use_hbm, gain_hbm,
     solved_ref, band_ref,
     X, fir_ref, chan_ref, use_ref, gain_ref,
-    Fa, Fb, Ta, Tb, acc, hi, lo, wide, msgs, both, turned,
+    Fa, Fb, Ta, Tb, acc, hi, lo, wide, msgs, turned,
     pw, pz, mysol, sol, splat, planes, fit, fit_out,
-    in_sem, arg_sem, core_send, core_recv, own_sem, turn_send, turn_recv, self_sem,
+    in_sem, arg_sem, turn_send, turn_recv, self_sem,
     pw_send, pw_recv, pz_send, pz_recv,
     sol_send, sol_recv, z_send, z_recv, fit_send, fit_recv, ready,
 ):
@@ -91,21 +101,22 @@
     def greet(chip, core):
         pl.semaphore_signal(barrier, inc=1, device_id=(chip, core), device_id_type=MESH)
 
-    def greet_plane(i):
-        t = lax.rem(xy * 2 + r + 1 + i, 2 * PLANE)
-        greet(t // 2 * NZ + z, lax.rem(t, 2))
-
-    loop(greet_plane, 2 * PLANE - 1)
-    loop(lambda i: greet(xy * NZ + lax.rem(z + 1 + i, NZ), r), NZ - 1)
+    def plane_chips():
+        return [lax.rem(x + dx, NX) * NY + lax.rem(y + dy, NY) for dx, dy in PLANE_ORDER]
+
+    for t in plane_chips()[:-1]:
+        greet(t * NZ + z, 0)
+        greet(t * NZ + z, 1)
+    greet(g, 1 - r)
+    for d in far_first(NZ)[:-1]:
+        greet(xy * NZ + lax.rem(z + d, NZ), r)
 
     def plane_is_here():
         pl.semaphore_wait(barrier, 2 * PLANE - 1 + NZ - 1)
-        loop(
-            lambda i: pl.semaphore_signal(
-                ready, inc=1, device_id=(xy * NZ + lax.rem(z + 1 + i, NZ), r), device_id_type=MESH
-            ),
-            NZ - 1,
-        )
+        for d in far_first(NZ)[:-1]:
+            pl.semaphore_signal(
+                ready, inc=1, device_id=(xy * NZ + lax.rem(z + d, NZ), r), device_id_type=MESH
+            )
 
     args[0].wait()
     chan = chan_ref[...]
@@ -212,71 +223,71 @@
         power = jnp.sum(jnp.sum(q * q, axis=1, keepdims=True), axis=0, keepdims=True)
         powers = jnp.where((sub8 == power_row) & (lane8 == power_lane + p), power, powers)
         spectra.append(v)
-    pw[xy * 2 + r] = powers * f32(1.0 / (SPEC * KEPT))
+    pz[z] = powers * f32(1.0 / (SPEC * KEPT))
     pl.semaphore_wait(ready, NZ - 1)
 
     def send_plane(source, buf, send, recv):
-        def one(i):
-            t = lax.rem(xy * 2 + r + 1 + i, 2 * PLANE)
-            core = lax.rem(t, 2)
+        def one(chip, core):
             pltpu.make_async_remote_copy(
                 src_ref=source(core), dst_ref=buf.at[xy * 2 + r], send_sem=send, recv_sem=recv,
-                device_id=(t // 2 * NZ + z, core), device_id_type=MESH,
+                device_id=(chip, core), device_id_type=MESH,
             ).start()
 
-        loop(one, 2 * PLANE - 1)
+        for t in plane_chips()[:-1]:
+            one(t * NZ + z, 0)
+            one(t * NZ + z, 1)
+        one(g, 1 - r)
 
     def send_z(buf, send, recv):
-        def one(i):
-            t = lax.rem(z + 1 + i, NZ)
+        for d in far_first(NZ)[:-1]:
             pltpu.make_async_remote_copy(
                 src_ref=buf.at[z], dst_ref=buf.at[z], send_sem=send, recv_sem=recv,
-                device_id=(xy * NZ + t, r), device_id_type=MESH,
+                device_id=(xy * NZ + lax.rem(z + d, NZ), r), device_id_type=MESH,
             ).start()
-
-        loop(one, NZ - 1)
 
     def drain(buf, n, sem):
         pltpu.make_async_copy(buf.at[pl.ds(0, n)], buf.at[pl.ds(0, n)], sem).wait()
 
-    send_plane(lambda core: pw.at[xy * 2 + r], pw, pw_send, pw_recv)
+    send_z(pz, pz_send, pz_recv)
 
     for p in range(4):
         wide[pl.ds(p, KEPT, stride=4), :] = spectra[p].T
     msgs.reshape(KEPT * 4, 128)[...] = wide[...].astype(bf)
-    core_copy = pltpu.make_async_remote_copy(
-        src_ref=msgs.at[:, 1 - r], dst_ref=both.at[:, r], send_sem=core_send, recv_sem=core_recv,
-        device_id=(g, 1 - r), device_id_type=MESH,
-    )
-    core_copy.start()
-    own_copy = pltpu.make_async_copy(msgs.at[:, r], both.at[:, r], own_sem)
-    own_copy.start()
-    own_copy.wait()
-    core_copy.wait_recv()
+    me = 2 * g + r
+
+    def send_block(t):
+        pltpu.make_async_remote_copy(
+            src_ref=msgs.at[t], dst_ref=turned.at[me], send_sem=turn_send, recv_sem=turn_recv,
+            device_id=(t // 2, lax.rem(t, 2)), device_id_type=MESH,
+        ).start()
 
     def send_chip(t):
-        pltpu.make_async_remote_copy(
-            src_ref=both.at[t], dst_ref=turned.at[g], send_sem=turn_send, recv_sem=turn_recv,
-            device_id=(t, r), device_id_type=MESH,
-        ).start()
+        for core in range(2):
+            pltpu.make_async_remote_copy(
+                src_ref=msgs.at[2 * t + core], dst_ref=turned.at[me], send_sem=turn_send, recv_sem=turn_recv,
+                device_id=(t, core), device_id_type=MESH,
+            ).start()
 
     def send_level(k):
-        pz_ = lax.rem(z + NZ // 2 + (1 - 2 * lax.rem(k, 2)) * ((k + 1) // 2), NZ)
+        far = lax.rem(z + NZ // 2 + (1 - 2 * lax.rem(k, 2)) * ((k + 1) // 2), NZ)
         for m in range(PLANE):
-            send_chip(lax.rem(xy + PLANE // 2 + m, PLANE) * NZ + pz_)
-
-    loop(send_level, NZ - 1)
+            send_chip(lax.rem(xy + PLANE // 2 + m, PLANE) * NZ + far)
+
+    loop(send_level, NZ - 2)
+
+    drain(pz, NZ - 1, pz_recv)
+    t = pz[0]
+    for i in range(1, NZ):
+        t = t + pz[i]
+    pw[xy * 2 + r] = t
+    send_plane(lambda core: pw.at[xy * 2 + r], pw, pw_send, pw_recv)
+
+    send_level(NZ - 2)
     for m in range(1, PLANE):
         send_chip(lax.rem(xy + m, PLANE) * NZ + z)
-    self_copy = pltpu.make_async_copy(both.at[g], turned.at[g], self_sem)
+    send_block(2 * g + 1 - r)
+    self_copy = pltpu.make_async_copy(msgs.at[me], turned.at[me], self_sem)
     self_copy.start()
-
-    drain(pw, 2 * PLANE - 1, pw_recv)
-    t = pw[0]
-    for i in range(1, 2 * PLANE):
-        t = t + pw[i]
-    pz[z] = t
-    send_z(pz, pz_send, pz_recv)
 
     u = chan.astype(f32) * f32(2.0 / (CHAN - 1)) - 1.0
     poly = [jnp.ones_like(u), u]
@@ -308,17 +319,17 @@
     for i in range(2 * PLANE):
         splat[i] = jnp.broadcast_to(column(i // 2 * (2 * NZ) + z * 2 + i % 2), (POLY, 128))
 
-    drain(pz, NZ - 1, pz_recv)
-    t = pz[0]
-    for i in range(1, NZ):
-        t = t + pz[i]
+    drain(pw, 2 * PLANE - 1, pw_recv)
+    t = pw[0]
+    for i in range(1, 2 * PLANE):
+        t = t + pw[i]
     t = lax.rsqrt(t + f32(1e-06))
     scale = jnp.concatenate([t[j : j + 1, :] for j in range(8)], axis=1)
 
     args[2].wait()
     args[3].wait()
     self_copy.wait()
-    drain(turned, CHIPS - 1, turn_recv)
+    drain(turned, 2 * CHIPS - 1, turn_recv)
 
     eye = (
         lax.broadcasted_iota(jnp.int32, (128, 128), 0) == lax.broadcasted_iota(jnp.int32, (128, 128), 1)
@@ -351,7 +362,7 @@
         t = jnp.zeros((8, 128), f32)
         for j in range(8):
             t = jnp.where(sub8 == j, jnp.broadcast_to(v[:, j * 128 : (j + 1) * 128], (8, 128)), t)
-        mysol[i] = t
+        mysol[i] = t.astype(bf)
 
     send_plane(lambda core: mysol.at[core], sol, sol_send, sol_recv)
     sol[xy * 2 + r] = mysol[r]
@@ -360,7 +371,7 @@
     for k in range(POLY):
         m = None
         for i in range(2 * PLANE):
-            t = sol[i] * splat[i, k : k + 1, :]
+            t = sol[i].astype(f32) * splat[i, k : k + 1, :]
             m = t if m is None else m + t
         part.append(m)
     part = jnp.concatenate(part, axis=0)
@@ -389,13 +400,20 @@
         for j in range(8):
             band_ref[i : i + 1, j * 128 : (j + 1) * 128] = fit[i, j : j + 1, :]
 
-    core_copy.wait_send()
-    drain(both, CHIPS - 1, turn_send)
+    drain(msgs, 2 * CHIPS - 1, turn_send)
     drain(pw, 2 * PLANE - 1, pw_send)
     drain(pz, NZ - 1, pz_send)
     drain(sol, 2 * PLANE - 1, sol_send)
     drain(planes, NZ - 1, z_send)
     fit_copy.wait_send()
+
+
+def emit(a_ref, b_ref, c_ref, d_ref, sem):
+    copies = [pltpu.make_async_copy(a_ref, c_ref, sem.at[0]), pltpu.make_async_copy(b_ref, d_ref, sem.at[1])]
+    for c in copies:
+        c.start()
+    for c in copies:
+        c.wait()
 
 
 def per_device(samples, fir_coeffs, kept_channels, usable, initial_gains):
@@ -424,13 +442,12 @@
             pltpu.VMEM((2, QT, KEPT), f32),
             pltpu.VMEM((2, 128, KEPT), f32),
             pltpu.VMEM((4 * KEPT, 128), f32),
-            pltpu.VMEM((CHIPS, 2, 4, 128), bf),
-            pltpu.VMEM((CHIPS, 2, 4, 128), bf),
-            pltpu.VMEM((CHIPS, 2, 4, 128), bf),
+            pltpu.VMEM((2 * CHIPS, 4, 128), bf),
+            pltpu.VMEM((2 * CHIPS, 4, 128), bf),
             pltpu.VMEM((2 * PLANE, 8, 128), f32),
             pltpu.VMEM((NZ, 8, 128), f32),
-            pltpu.VMEM((2, 8, 128), f32),
-            pltpu.VMEM((2 * PLANE, 8, 128), f32),
+            pltpu.VMEM((2, 8, 128), bf),
+            pltpu.VMEM((2 * PLANE, 8, 128), bf),
             pltpu.VMEM((2 * PLANE + 2, POLY, 128), f32),
             pltpu.VMEM((NZ, POLY * 8, 128), bf),
             pltpu.VMEM((2, 8, 128), f32),
@@ -438,12 +455,21 @@
             dma((CHUNKS, 4)),
             dma((4,)),
         ]
-        + [dma] * 16
+        + [dma] * 13
         + [pltpu.SemaphoreType.REGULAR],
         compiler_params=pltpu.CompilerParams(
             collective_id=0, has_side_effects=True, vmem_limit_bytes=60 * 2**20
         ),
     )(tiles, coeffs, chan, usable.reshape(1, INPUTS), initial_gains.reshape(2, INPUTS))
+    solved, band = pl.pallas_call(
+        emit,
+        name="emit",
+        out_shape=[jax.ShapeDtypeStruct((2, INPUTS), f32)] * 2,
+        in_specs=[pl.BlockSpec(memory_space=pltpu.HBM)] * 2,
+        out_specs=[pl.BlockSpec(memory_space=pltpu.HBM)] * 2,
+        scratch_shapes=[dma((2,))],
+        compiler_params=pltpu.CompilerParams(vmem_limit_bytes=60 * 2**20),
+    )(solved, band)
     return solved.reshape(1, 2, INPUTS), band.reshape(1, 2, INPUTS)
 
 

time: 48.7 us -> 45.1 us (0.926)
  local copies, waits for them, and re-layouts: 2.59 us -> 0 us
  Pallas kernels: 45.2 us -> 44.4 us
    unnamed x2 -> x0, local copies, waits for them, and re-layouts: 2.59 us -> none
    pallas_call x1, Pallas kernels: 45.2 us -> 42.8 us  [per_device(): pl.pallas_call(kernel, name='fx_calibrate', out_shape=[jax.ShapeDtypeStru...]
    pallas_call x0 -> x1, Pallas kernels: none -> 1.62 us  [per_device(): pl.pallas_call(emit, name='emit', out_shape=[jax.ShapeDtypeStruct((2, INP...]
where the time goes in v3:
time: 45.1 us
  Pallas kernels  44.4 us (98%)
  between operations  0.64 us (1%)
    pallas_call x1, Pallas kernels, per_device(): pl.pallas_call(kernel, name='fx_calibrate', out_shape=[jax.ShapeDtypeStru...  42.8 us
    pallas_call x1, Pallas kernels, per_device(): pl.pallas_call(emit, name='emit', out_shape=[jax.ShapeDtypeStruct((2, INP...  1.62 us

profile of v3, /device:TPU:1, one launch (start us, length us, event | category | flops | bytes accessed | tf_op | source)
XLA Modules:
  0.0 45.1 jit_solution(18140507432584990016)
XLA Ops:
  0.6 42.8 %fx_calibrate.1 = (f32[2,1024]{1,0:T(2,128)}, f32[2,1024]{1,0:T(2,128)}) custom-call(bf16[8576,4,128]{2,1,0:T(4,128)(2,1)} %bitcast.11, f32[128,4,128]{2,1,0:T(4,128)} %bitcast.12, s32[1,256]{1,0:T(1,128)} %bitcast.15, s32[1,1024]{1,0:T(1,128)} %bitcast.14, f32[2,1024]{1,0:T(2,128)} %bitcast.13), custom_call_target="tpu_custom_call" | custom-call | tf_op jit(solution)/shard_map/fx_calibrate/pallas_call | solution.py:425
  43.4 1.6 %emit.1 = (f32[2,1024]{1,0:T(2,128)}, f32[2,1024]{1,0:T(2,128)}) custom-call(f32[2,1024]{1,0:T(2,128)} %get-tuple-element.6.a_ref, f32[2,1024]{1,0:T(2,128)} %get-tuple-element.7.b_ref), custom_call_target="tpu_custom_call" | custom-call | tf_op jit(solution)/shard_map/emit/pallas_call | solution.py:464

commit v4 on v3

--- a/solution.py
+++ b/solution.py
@@ -23,8 +23,9 @@
 PLANE = NX * NY
 TILES = NFFT // 128
 QT = TILES // 4
-CHUNKS = 8
-KC = QT // CHUNKS
+KC = 4
+EDGE = 2
+CHUNKS = (QT - 2 * EDGE) // KC
 
 
 def turns(phase):
@@ -78,9 +79,15 @@
 
     src = x_hbm.reshape(FRAMES, 4, QT, 4, 128)
 
-    def sample_copy(k, j):
-        at = pl.ds(KC * k, KC)
-        return pltpu.make_async_copy(src.at[:, j, at], X.at[:, at, j], in_sem.at[k, j])
+    def sample_copies(k, first, tiles):
+        at = pl.ds(first, tiles)
+        return [pltpu.make_async_copy(src.at[:, j, at], X.at[:, at, j], in_sem.at[k, j]) for j in range(4)]
+
+    def chunk(k):
+        return sample_copies(k + 1, EDGE + KC * k, KC)
+
+    head = sample_copies(0, 0, EDGE)
+    tail = sample_copies(CHUNKS + 1, QT - EDGE, EDGE)
 
     args = [
         pltpu.make_async_copy(a, b, arg_sem.at[i])
@@ -90,9 +97,8 @@
     ]
     args[0].start()
     args[1].start()
-    for k in range(CHUNKS):
-        for j in range(4):
-            sample_copy(k, j).start()
+    for copy in sum([head] + [chunk(k) for k in range(CHUNKS)] + [tail], []):
+        copy.start()
     args[2].start()
     args[3].start()
 
@@ -140,8 +146,8 @@
     rows = X.reshape(FRAMES, QT, 16, 128)
     quarter = lax.broadcasted_iota(jnp.int32, (16, 128), 0) // 4
 
-    def fir(k, h, F, T):
-        kk = KC * k + h
+    def fir(first, h, F, T):
+        kk = first + h
         static = isinstance(h, int)
         col = slice(h * 128, h * 128 + 128) if static else pl.ds(pl.multiple_of(h * 128, 128), 128)
         coef = []
@@ -166,36 +172,43 @@
             T[0, row, :] = (hr * lr - hm * lm).astype(bf)
             T[1, row, :] = (hr * lm + hm * lr).astype(bf)
 
-    def mm(F, T):
+    def mm(F, T, tiles=KC, first=False):
+        depth = tiles * 128
         for n in range(2):
-            d = jnp.dot(F[...], T[n], preferred_element_type=f32)
+            d = jnp.dot(F[:, 0:depth], T[n, 0:depth, :], preferred_element_type=f32)
             for q in range(2):
-                acc[2 * n + q] += d[:, q * 128 : (q + 1) * 128]
-
-    def wait_samples(k):
-        for j in range(4):
-            sample_copy(k, j).wait()
-
-    def stage(k, prev, cur):
-        wait_samples(k)
-        mm(*prev)
+                if first:
+                    acc[2 * n + q] = d[:, q * 128 : (q + 1) * 128]
+                else:
+                    acc[2 * n + q] += d[:, q * 128 : (q + 1) * 128]
+
+    def wait(copies):
+        for copy in copies:
+            copy.wait()
+
+    def stage(k, prev, cur, **kw):
+        wait(chunk(k))
+        mm(*prev, **kw)
         for h in range(KC):
-            fir(k, h, *cur)
+            fir(EDGE + KC * k, h, *cur)
 
     A, B = (Fa, Ta), (Fb, Tb)
-    acc[...] = jnp.zeros_like(acc)
     args[1].wait()
-    wait_samples(0)
-    loop(lambda h: fir(0, h, *A), KC)
+    wait(head)
+    loop(lambda h: fir(0, h, *A), EDGE)
+    stage(0, A, B, tiles=EDGE, first=True)
 
     def pair(i):
         pl.when(i == CHUNKS // 2 - 2)(plane_is_here)
-        stage(2 * i + 1, A, B)
-        stage(2 * i + 2, B, A)
-
-    loop(pair, CHUNKS // 2 - 1)
-    stage(CHUNKS - 1, A, B)
+        stage(2 * i + 1, B, A)
+        stage(2 * i + 2, A, B)
+
+    loop(pair, CHUNKS // 2)
+    wait(tail)
     mm(*B)
+    for h in range(EDGE):
+        fir(QT - EDGE, h, *A)
+    mm(*A, tiles=EDGE)
 
     quads = []
     for j in range(4):
@@ -425,7 +438,7 @@
     solved, band = pl.pallas_call(
         kernel,
         name="fx_calibrate",
-        out_shape=[jax.ShapeDtypeStruct((2, INPUTS), f32)] * 2,
+        out_shape=[pltpu.VMEM((2, INPUTS), f32)] * 2,
         in_specs=[pl.BlockSpec(memory_space=pltpu.HBM)] * 5,
         out_specs=[vmem] * 2,
         scratch_shapes=[
@@ -452,7 +465,7 @@
             pltpu.VMEM((NZ, POLY * 8, 128), bf),
             pltpu.VMEM((2, 8, 128), f32),
             pltpu.VMEM((8, 128), f32),
-            dma((CHUNKS, 4)),
+            dma((CHUNKS + 2, 4)),
             dma((4,)),
         ]
         + [dma] * 13
@@ -465,10 +478,10 @@
         emit,
         name="emit",
         out_shape=[jax.ShapeDtypeStruct((2, INPUTS), f32)] * 2,
-        in_specs=[pl.BlockSpec(memory_space=pltpu.HBM)] * 2,
+        in_specs=[pl.BlockSpec(memory_space=pltpu.VMEM)] * 2,
         out_specs=[pl.BlockSpec(memory_space=pltpu.HBM)] * 2,
         scratch_shapes=[dma((2,))],
-        compiler_params=pltpu.CompilerParams(vmem_limit_bytes=60 * 2**20),
+        compiler_params=pltpu.CompilerParams(vmem_limit_bytes=2**20),
     )(solved, band)
     return solved.reshape(1, 2, INPUTS), band.reshape(1, 2, INPUTS)
 

time: 45.1 us -> 43.5 us (0.965)
  Pallas kernels: 44.4 us -> 42.7 us
    pallas_call x1, Pallas kernels: 1.62 us -> 0.62 us  [per_device(): pl.pallas_call(emit, name='emit', out_shape=[jax.ShapeDtypeStruct((2, INP...]
    pallas_call x1, Pallas kernels: 42.8 us -> 42.1 us  [per_device(): pl.pallas_call(kernel, name='fx_calibrate', out_shape=[pltpu.VMEM((2, INP...]
where the time goes in v4:
time: 43.5 us; the launch traced here: 43.4 us
  Pallas kernels  42.7 us (98%)
  between operations  0.64 us (1%)
    pallas_call x1, Pallas kernels, per_device(): pl.pallas_call(kernel, name='fx_calibrate', out_shape=[pltpu.VMEM((2, INP...  42.1 us

profile of v4, /device:TPU:1, one launch (start us, length us, event | category | flops | bytes accessed | tf_op | source)
XLA Modules:
  0.0 43.4 jit_solution(2946083816910618684)
XLA Ops:
  0.6 42.1 %fx_calibrate.1 = (f32[2,1024]{1,0:T(2,128)S(1)}, f32[2,1024]{1,0:T(2,128)S(1)}) custom-call(bf16[8576,4,128]{2,1,0:T(4,128)(2,1)} %bitcast.11, f32[128,4,128]{2,1,0:T(4,128)} %bitcast.12, s32[1,256]{1,0:T(1,128)} %bitcast.15, s32[1,1024]{1,0:T(1,128)} %bitcast.14, f32[2,1024]{1,0:T(2,128)} %bitcast.13), custom_call_target="tpu_custom_call" | custom-call | tf_op jit(solution)/shard_map/fx_calibrate/pallas_call | solution.py:438
  42.8 0.6 %emit.1 = (f32[2,1024]{1,0:T(2,128)}, f32[2,1024]{1,0:T(2,128)}) custom-call(f32[2,1024]{1,0:T(2,128)S(1)} %get-tuple-element.6.a_ref, f32[2,1024]{1,0:T(2,128)S(1)} %get-tuple-element.7.b_ref), custom_call_target="tpu_custom_call" | custom-call | tf_op jit(solution)/shard_map/emit/pallas_call | solution.py:477

commit v5 on v4

--- a/solution.py
+++ b/solution.py
@@ -218,8 +218,8 @@
         quads.append((rr, ri))
     sub8 = lax.broadcasted_iota(jnp.int32, (8, 128), 0)
     lane8 = lax.broadcasted_iota(jnp.int32, (8, 128), 1)
-    power_row, power_lane = xy // 2, lax.rem(xy, 2) * 64 + z * 8 + r * 4
-    powers = jnp.zeros((8, 128), f32)
+    power_lane = lax.rem(xy, 2) * 64 + z * 8 + r * 4
+    powers = jnp.zeros((1, 128), f32)
     spectra = []
     for p in range(4):
         sr = si = None
@@ -234,7 +234,7 @@
         v = jnp.concatenate([sr, si], axis=0)
         q = v.astype(bf).astype(f32)
         power = jnp.sum(jnp.sum(q * q, axis=1, keepdims=True), axis=0, keepdims=True)
-        powers = jnp.where((sub8 == power_row) & (lane8 == power_lane + p), power, powers)
+        powers = jnp.where(lane8[0:1] == power_lane + p, power, powers)
         spectra.append(v)
     pz[z] = powers * f32(1.0 / (SPEC * KEPT))
     pl.semaphore_wait(ready, NZ - 1)
@@ -333,11 +333,8 @@
         splat[i] = jnp.broadcast_to(column(i // 2 * (2 * NZ) + z * 2 + i % 2), (POLY, 128))
 
     drain(pw, 2 * PLANE - 1, pw_recv)
-    t = pw[0]
-    for i in range(1, 2 * PLANE):
-        t = t + pw[i]
-    t = lax.rsqrt(t + f32(1e-06))
-    scale = jnp.concatenate([t[j : j + 1, :] for j in range(8)], axis=1)
+    scale = jnp.concatenate([pw[4 * j] + pw[4 * j + 1] + pw[4 * j + 2] + pw[4 * j + 3] for j in range(8)], axis=1)
+    scale = lax.rsqrt(scale + f32(1e-06))
 
     args[2].wait()
     args[3].wait()
@@ -457,8 +454,8 @@
             pltpu.VMEM((4 * KEPT, 128), f32),
             pltpu.VMEM((2 * CHIPS, 4, 128), bf),
             pltpu.VMEM((2 * CHIPS, 4, 128), bf),
-            pltpu.VMEM((2 * PLANE, 8, 128), f32),
-            pltpu.VMEM((NZ, 8, 128), f32),
+            pltpu.VMEM((2 * PLANE, 1, 128), f32),
+            pltpu.VMEM((NZ, 1, 128), f32),
             pltpu.VMEM((2, 8, 128), bf),
             pltpu.VMEM((2 * PLANE, 8, 128), bf),
             pltpu.VMEM((2 * PLANE + 2, POLY, 128), f32),

time: 43.5 us -> 43.1 us (level)
  no operation moved by 1% of the time
where the time goes in v5:
time: 43.1 us; the launch traced here: 43 us
  Pallas kernels  42.4 us (98%)
  between operations  0.64 us (1%)
    pallas_call x1, Pallas kernels, per_device(): pl.pallas_call(kernel, name='fx_calibrate', out_shape=[pltpu.VMEM((2, INP...  41.8 us

profile of v5, /device:TPU:1, one launch (start us, length us, event | category | flops | bytes accessed | tf_op | source)
XLA Modules:
  0.0 43.0 jit_solution(14747340838554433464)
XLA Ops:
  0.6 41.8 %fx_calibrate.1 = (f32[2,1024]{1,0:T(2,128)S(1)}, f32[2,1024]{1,0:T(2,128)S(1)}) custom-call(bf16[8576,4,128]{2,1,0:T(4,128)(2,1)} %bitcast.11, f32[128,4,128]{2,1,0:T(4,128)} %bitcast.12, s32[1,256]{1,0:T(1,128)} %bitcast.15, s32[1,1024]{1,0:T(1,128)} %bitcast.14, f32[2,1024]{1,0:T(2,128)} %bitcast.13), custom_call_target="tpu_custom_call" | custom-call | tf_op jit(solution)/shard_map/fx_calibrate/pallas_call | solution.py:435
  42.4 0.6 %emit.1 = (f32[2,1024]{1,0:T(2,128)}, f32[2,1024]{1,0:T(2,128)}) custom-call(f32[2,1024]{1,0:T(2,128)S(1)} %get-tuple-element.6.a_ref, f32[2,1024]{1,0:T(2,128)S(1)} %get-tuple-element.7.b_ref), custom_call_target="tpu_custom_call" | custom-call | tf_op jit(solution)/shard_map/emit/pallas_call | solution.py:474
